TPU v7x, 256 devices: a whole 4x4x8 slice. The times are simulated.
256 devices in a mesh: node: 16 (over x, y_lo, core), tm: 16 (over y_hi, z).
Axes of the slice: x: 4, y: 4 (y_hi: 2, y_lo: 2; y = y_hi * 2 + y_lo), z: 8, core: 2. Of those that a mesh axis runs over, the one named last changes fastest.
Arguments:
- series: bfloat16 [48, 4096, 256], P(None, ('node', 'tm')), may hold values from -16 to 16
- t_query: bfloat16 [256, 256], replicated, may hold values from -1 to 1
- t_key: bfloat16 [256, 256], replicated, may hold values from -5 to 5
- t_value: bfloat16 [256, 256], replicated, may hold values from -0.375 to 0.375
- t_out: bfloat16 [256, 256], replicated, may hold values from -0.375 to 0.375
- s_query: bfloat16 [256, 256], replicated, may hold values from -1 to 1
- s_key: bfloat16 [256, 256], replicated, may hold values from -5 to 5
- s_value: bfloat16 [256, 256], replicated, may hold values from -0.375 to 0.375
- s_out: bfloat16 [256, 256], replicated, may hold values from -0.375 to 0.375
- gain_first: float32 [256], replicated, may hold values from 0.25 to 1.75
- gain_second: float32 [256], replicated, may hold values from 0.25 to 1.75
Outputs:
- output: bfloat16 [48, 4096, 256], P(None, ('node', 'tm'))
All inputs are finite; a program needn't handle non-finite values.
Results may differ from a plain program's by a relative error of at most 0.0092.
Values may be sent and summed in bfloat16 or wider, within the bound.
A program may use at most 64 MiB of HBM per device.

v0:
```python
import math

import jax
import jax.numpy as jnp
from jax import lax
from jax.experimental import pallas as pl
from jax.experimental.pallas import tpu as pltpu
from jax.sharding import PartitionSpec as P

HEADS = 8
epsilon = 1e-05
f32, bf16 = jnp.float32, jnp.bfloat16
MESH = pl.DeviceIdType.MESH
GROUPS = 16
BLOCK_SLOTS = 16


def layer_norm(values, gain):
    center = values - jnp.mean(values, axis=-1, keepdims=True)
    spread = jnp.mean(center * center, axis=-1, keepdims=True)
    return center * lax.rsqrt(spread + epsilon) * gain


def dot_t(a, b):
    return lax.dot_general(a, b, (((1,), (1,)), ((), ())), preferred_element_type=f32)


def dot(a, b):
    return jnp.dot(a, b, preferred_element_type=f32)


def wide(column, count):
    return jnp.concatenate([column] * count, axis=1)


def block_kernel(
    *refs,
):
    operands, refs = refs[:11], refs[11:]
    staged, refs = refs[1:12], (refs[0],) + refs[12:]
    body(operands, staged, *refs)


def body(
    operands, staged, out, load_sem, keep_sem,
    flat_q, flat_k, flat_v, flat_mix, hid,
    keys_in, k_buf, v_buf, q_mask, acc, row_max, result,
    a_send, a_recv, n_send, n_recv, s_send, s_recv, r_send, r_recv,
):
    series, tq, tk, tv, to, wq, wk, wv, wo, gain_first, gain_second = staged
    steps, rows, width = keys_in.shape
    window, slab, _ = series.shape
    block = rows // BLOCK_SLOTS
    half = width // 2
    head_dim = width // HEADS
    scale = math.log2(math.e) / math.sqrt(head_dim)
    node = lax.axis_index("node")
    me = lax.axis_index("tm")
    core = node % 2
    y_lo = (node // 2) % 2
    x = node // 4
    sibling = node + 1 - 2 * core
    y_peer = node + 2 - 4 * y_lo
    right = ((x + 1) % 4) * 4 + node % 4
    left = ((x + 3) % 4) * 4 + node % 4

    def load(i):
        return pltpu.make_async_copy(operands[i], staged[i], load_sem.at[i])

    for i in range(len(operands)):
        load(i).start()
    barrier = pltpu.get_barrier_semaphore()
    for other in (sibling, y_peer, right, left):
        pl.semaphore_signal(barrier, inc=1, device_id={"node": other}, device_id_type=MESH)

    def greet(k, carry):
        pl.semaphore_signal(
            barrier, inc=1, device_id={"tm": (me + k) % GROUPS}, device_id_type=MESH
        )
        return carry

    lax.fori_loop(1, GROUPS, greet, 0)

    for i in range(4):
        load(i).wait()
    flat = series[...].reshape(window * slab, width)
    for s in range(2):
        cut = pl.ds(s * half, half)
        flat_q[s] = dot(flat, tq[:, cut]).astype(bf16).astype(f32)
        flat_k[s] = dot(flat, tk[:, cut]).astype(bf16).astype(f32)
        flat_v[s] = dot(flat, tv[:, cut]).astype(bf16).astype(f32)
    per = 4
    span = per * window
    row_id = lax.broadcasted_iota(jnp.int32, (span, span), 0)
    col_id = lax.broadcasted_iota(jnp.int32, (span, span), 1)

    def owner(index):
        total = jnp.zeros_like(index)
        for k in range(1, per):
            total = total + (index >= k * window).astype(jnp.int32)
        return total

    seen = (row_id >= col_id) & (owner(row_id) == owner(col_id))
    lane = lax.broadcasted_iota(jnp.int32, (span, width), 1) // head_dim
    half_lane = lax.broadcasted_iota(jnp.int32, (span, half), 1) // head_dim
    ones = jnp.ones((span, half), bf16)
    for g in range(slab // per):
        def gather(ref):
            sides = []
            for s in range(2):
                parts = [
                    ref[s, pl.ds(g * per + i, window, stride=slab), :].astype(bf16)
                    for i in range(per)
                ]
                sides.append(jnp.concatenate(parts, axis=0))
            return jnp.concatenate(sides, axis=1)

        q, k, v = gather(flat_q), gather(flat_k), gather(flat_v)
        for s in range(2):
            values = jnp.concatenate([v[:, s * half : (s + 1) * half], ones], axis=1)
            mixed = jnp.zeros((span, half), f32)
            for i in range(HEADS // 2):
                h = s * (HEADS // 2) + i
                scores = dot_t(jnp.where(lane == h, q, jnp.zeros_like(q)), k)
                scores = jnp.where(seen, scores, -1e30)
                top = jnp.max(scores, axis=1, keepdims=True)
                p = jnp.exp2((scores - top) * scale).astype(bf16)
                a = dot(p, values)
                mixed = jnp.where(half_lane == i, a[:, :half] / a[:, half:], mixed)
            for i in range(per):
                flat_mix[s, pl.ds(g * per + i, window, stride=slab), :] = mixed[
                    i * window : (i + 1) * window
                ]
    for i in range(4, len(operands)):
        load(i).wait()
    mixed = jnp.concatenate([flat_mix[0].astype(bf16), flat_mix[1].astype(bf16)], axis=1)
    first = flat.astype(f32) + dot(mixed, to[...])
    hid[...] = layer_norm(first, gain_first[...]).astype(bf16).reshape(window, slab, width)

    pl.semaphore_wait(barrier, GROUPS - 1 + 4)

    my_rows = pl.ds(pl.multiple_of(me * slab, slab), slab)

    def scatter(t):
        def one(k, carry):
            j = (me + k) % GROUPS
            pltpu.make_async_remote_copy(
                src_ref=hid.at[steps * j + t],
                dst_ref=keys_in.at[t, my_rows, :],
                send_sem=a_send.at[t],
                recv_sem=a_recv.at[t],
                device_id={"tm": j},
                device_id_type=MESH,
            ).start()
            return carry

        lax.fori_loop(1, GROUPS, one, 0)

    for t in range(steps):
        scatter(t)
    for t in range(steps):
        keys_in[t, my_rows, :] = hid[steps * me + t]

    def wait_bytes(ref, sem):
        pltpu.make_async_copy(ref, ref, sem).wait()

    cut = block // 2
    routes = [
        (0, 2 * block, block, y_peer),
        (0, 3 * block, block, right),
        (0, 4 * block, block, left),
        (2 * block, 8 * block, block, right),
        (2 * block, 9 * block, block, left),
        (3 * block, 10 * block, cut, right),
        (4 * block + cut, 10 * block + cut, cut, left),
        (8 * block, 11 * block, cut, right),
        (9 * block + cut, 11 * block + cut, cut, left),
    ]
    shares = [(0, 1, 1), (2, 5, 3), (8, 12, 2), (10, 14, 2)]

    def route(t, i):
        src, dst, count, other = routes[i]
        return pltpu.make_async_remote_copy(
            src_ref=keys_in.at[t, pl.ds(src, count), :],
            dst_ref=keys_in.at[t, pl.ds(dst, count), :],
            send_sem=n_send.at[t, i],
            recv_sem=n_recv.at[t, i],
            device_id={"node": other},
            device_id_type=MESH,
        )

    def share(t, i):
        src, dst, count = shares[i]
        return pltpu.make_async_remote_copy(
            src_ref=keys_in.at[t, pl.ds(src * block, count * block), :],
            dst_ref=keys_in.at[t, pl.ds(dst * block, count * block), :],
            send_sem=s_send.at[t, i],
            recv_sem=s_recv.at[t, i],
            device_id={"node": sibling},
            device_id_type=MESH,
        )

    def own_ready(t):
        wait_bytes(keys_in.at[t, pl.ds(0, block - slab), :], a_recv.at[t])
        share(t, 0).start()
        for i in (1, 2, 0):
            route(t, i).start()

    def near_ready(t):
        for i in (0, 1, 2):
            route(t, i).wait_recv()
        for i in (3, 4, 5, 6):
            route(t, i).start()
        share(t, 1).start()

    def side_ready(t):
        for i in (3, 4):
            route(t, i).wait_recv()
        route(t, 7).start()
        route(t, 8).start()
        share(t, 2).start()

    def far_ready(t):
        for i in (5, 6, 7, 8):
            route(t, i).wait_recv()
        share(t, 3).start()

    def shared(t, i):
        share(t, i).wait_recv()

    chunk = k_buf.shape[1]
    v_buf[:, :, :, half:] = jnp.ones((2, 2, chunk, half), bf16)
    turn = [0]

    def project_queries(t):
        q = (dot(keys_in[t, pl.ds(0, block), :], wq[...]) * scale).astype(bf16)
        lane = lax.broadcasted_iota(jnp.int32, (block, width), 1) // head_dim
        for h in range(HEADS):
            q_mask[t, h] = jnp.where(lane == h, q, jnp.zeros_like(q))

    def attend(t, parts, fresh):
        slot = turn[0] % 2
        turn[0] += 1
        n = 0
        for start, count in parts:
            first_row = pl.multiple_of(start * block, block)
            rows_in = keys_in[t, pl.ds(first_row, count * block), :]
            here = pl.ds(n, count * block)
            k_buf[slot, here, :] = dot(rows_in, wk[...]).astype(bf16)
            v = dot(rows_in, wv[...]).astype(bf16)
            v_buf[slot, 0, here, :half] = v[:, :half]
            v_buf[slot, 1, here, :half] = v[:, half:]
            n += count * block
        for h in range(HEADS):
            s = dot_t(q_mask[t, h], k_buf[slot, :n, :])
            top = jnp.max(s, axis=1, keepdims=True)
            if fresh:
                new = jnp.broadcast_to(top, (block, 128))
            else:
                old = row_max[t, h]
                new = jnp.maximum(old, top)
            p = jnp.exp2(s - wide(new, n // 128)).astype(bf16)
            update = dot(p, v_buf[slot, h // 4, :n, :])
            if fresh:
                acc[t, h] = update
            else:
                fade = jnp.exp2(old - new)
                acc[t, h] = acc[t, h] * wide(fade, width // 128) + update
            row_max[t, h] = new

    def finish(t):
        lane = lax.broadcasted_iota(jnp.int32, (block, half), 1) // head_dim
        sides = []
        for s in range(2):
            mixed = jnp.zeros((block, half), f32)
            for i in range(HEADS // 2):
                a = acc[t, s * (HEADS // 2) + i]
                mixed = jnp.where(lane == i, a[:, :half] / a[:, half:], mixed)
            sides.append(mixed.astype(bf16))
        mixed = jnp.concatenate(sides, axis=1)
        second = keys_in[t, pl.ds(0, block), :].astype(f32) + dot(mixed, wo[...])
        result[t] = layer_norm(second, gain_second[...]).astype(bf16)

    def give(t):
        def one(k, carry):
            j = (me + k) % GROUPS
            pltpu.make_async_remote_copy(
                src_ref=result.at[t, pl.ds(pl.multiple_of(j * slab, slab), slab), :],
                dst_ref=out.at[steps * me + t],
                send_sem=r_send.at[t],
                recv_sem=r_recv.at[t],
                device_id={"tm": j},
                device_id_type=MESH,
            ).start()
            return carry

        lax.fori_loop(1, GROUPS, one, 0)

    def near(t):
        def one(i, carry):
            pl.when(i == 1)(lambda: shared(t, 1))
            attend(t, [(2 + 3 * i, 3)], False)
            return carry

        lax.fori_loop(0, 2, one, 0)

    def far(t, between):
        def one(i, carry):
            pl.when(i == 1)(between)
            attend(t, [(8 + 2 * i, 2), (12 + 2 * i, 2)], False)
            return carry

        lax.fori_loop(0, 2, one, 0)

    def turn_last():
        give(1)
        shared(2, 3)

    own_ready(0)
    own_ready(1)
    project_queries(0)
    shared(0, 0)
    attend(0, [(0, 2)], True)
    near_ready(0)
    own_ready(2)
    project_queries(1)
    near(0)
    shared(1, 0)
    attend(1, [(0, 2)], True)
    side_ready(0)
    near_ready(1)
    project_queries(2)
    near(1)
    shared(0, 2)
    attend(0, [(8, 2), (12, 2)], False)
    far_ready(0)
    shared(2, 0)
    attend(2, [(0, 2)], True)
    side_ready(1)
    near_ready(2)
    shared(0, 3)
    attend(0, [(10, 2), (14, 2)], False)
    finish(0)
    give(0)
    near(2)
    far_ready(1)
    side_ready(2)
    shared(1, 2)
    far(1, lambda: shared(1, 3))
    finish(1)
    far_ready(2)
    shared(2, 2)
    far(2, turn_last)
    finish(2)
    give(2)

    def keep(t):
        return pltpu.make_async_copy(
            result.at[t, my_rows, :], out.at[steps * me + t], keep_sem.at[t]
        )

    for t in range(steps):
        keep(t).start()
    for t in range(steps):
        keep(t).wait()
    for t in range(steps):
        wait_bytes(keys_in.at[t, pl.ds(0, block - slab), :], a_send.at[t])
        for i in range(len(routes)):
            route(t, i).wait_send()
        for i in range(len(shares)):
            share(t, i).wait_send()
        wait_bytes(result.at[t, pl.ds(0, block - slab), :], r_send.at[t])
        wait_bytes(result.at[t, pl.ds(0, block - slab), :], r_recv.at[t])


def shards(
    series, t_query, t_key, t_value, t_out, s_query, s_key, s_value, s_out, gain_first, gain_second
):
    window, slab, width = series.shape
    steps = window // GROUPS
    block = slab * GROUPS
    chunk = 4 * block
    hbm = pl.BlockSpec(memory_space=pltpu.HBM)
    weight = pltpu.VMEM((width, width), bf16)
    gain = pltpu.VMEM((1, width), f32)
    flat = pltpu.VMEM((2, window * slab, width // 2), f32)
    return pl.pallas_call(
        block_kernel,
        out_shape=jax.ShapeDtypeStruct(series.shape, bf16),
        in_specs=[hbm] * 11,
        out_specs=hbm,
        scratch_shapes=[
            pltpu.VMEM(series.shape, bf16),
            *[weight] * 8,
            gain,
            gain,
            pltpu.SemaphoreType.DMA((11,)),
            pltpu.SemaphoreType.DMA((steps,)),
            flat,
            flat,
            flat,
            flat,
            pltpu.VMEM((window, slab, width), bf16),
            pltpu.VMEM((steps, BLOCK_SLOTS * block, width), bf16),
            pltpu.VMEM((2, chunk, width), bf16),
            pltpu.VMEM((2, 2, chunk, width), bf16),
            pltpu.VMEM((steps, HEADS, block, width), bf16),
            pltpu.VMEM((steps, HEADS, block, width), f32),
            pltpu.VMEM((steps, HEADS, block, 128), f32),
            pltpu.VMEM((steps, block, width), bf16),
            pltpu.SemaphoreType.DMA((steps,)),
            pltpu.SemaphoreType.DMA((steps,)),
            pltpu.SemaphoreType.DMA((steps, 9)),
            pltpu.SemaphoreType.DMA((steps, 9)),
            pltpu.SemaphoreType.DMA((steps, 4)),
            pltpu.SemaphoreType.DMA((steps, 4)),
            pltpu.SemaphoreType.DMA((steps,)),
            pltpu.SemaphoreType.DMA((steps,)),
        ],
        compiler_params=pltpu.CompilerParams(
            collective_id=0, has_side_effects=True, vmem_limit_bytes=63 * 2**20
        ),
    )(
        series, t_query, t_key, t_value, t_out, s_query, s_key, s_value, s_out,
        gain_first.reshape(1, width), gain_second.reshape(1, width),
    )


def solution(mesh):
    in_specs = (P(None, ("node", "tm"), None), P(), P(), P(), P(), P(), P(), P(), P(), P(), P())
    out_specs = P(None, ("node", "tm"), None)
    return jax.shard_map(shards, mesh=mesh, in_specs=in_specs, out_specs=out_specs, check_vma=False)
```

profile of v0, /device:TPU:1, one launch (start us, length us, event | category | flops | bytes accessed | tf_op | source)
XLA Modules:
  0.0 73.5 jit_solution(10977635612979101352)
XLA Ops:
  0.0 71.7 %shard_map.109 = bf16[48,16,256]{2,1,0:T(8,128)(2,1)} custom-call(bf16[48,16,256]{2,1,0:T(8,128)(2,1)} %refs_0_.1, bf16[256,256]{1,0:T(8,128)(2,1)} %refs_1_.1, bf16[256,256]{1,0:T(8,128)(2,1)} %refs_2_.1, bf16[256,256]{1,0:T(8,128)(2,1)} %refs_3_.1, bf16[256,256]{1,0:T(8,128)(2,1)} %refs_4_.1, bf16[256,256]{1,0:T(8,128)(2,1)} %refs_5_.1, ...), custom_call_target="tpu_custom_call" | custom-call | tf_op jit(solution)/shard_map/pallas_call | solution.py:387
  71.7 1.8 %copy.13 = bf16[48,16,256]{2,1,0:T(8,128)(2,1)} copy(bf16[48,16,256]{2,1,0:T(8,128)(2,1)} %shard_map.109) | data formatting | bytes 786432
where the time goes:
time: 73.6 us; the launch traced here: 73.5 us
  Pallas kernels  71.7 us (97%)
  local copies, waits for them, and re-layouts  1.77 us (2%)
    pallas_call x1, Pallas kernels, shards(): pl.pallas_call(block_kernel, out_shape=jax.ShapeDtypeStruct(series.shape,...  71.7 us
    unnamed x1, local copies, waits for them, and re-layouts  1.77 us

commit v1 on v0

--- a/solution.py
+++ b/solution.py
@@ -44,7 +44,7 @@
 def body(
     operands, staged, out, load_sem, keep_sem,
     flat_q, flat_k, flat_v, flat_mix, hid,
-    keys_in, k_buf, v_buf, q_mask, acc, row_max, result,
+    keys_in, v_buf, q_mask, acc, row_max, result,
     a_send, a_recv, n_send, n_recv, s_send, s_recv, r_send, r_recv,
 ):
     series, tq, tk, tv, to, wq, wk, wv, wo, gain_first, gain_second = staged
@@ -139,6 +139,7 @@
 
     pl.semaphore_wait(barrier, GROUPS - 1 + 4)
 
+    far_first = (4, 12, 3, 13, 5, 11, 2, 14, 6, 10, 1, 15, 7, 9, 8)
     my_rows = pl.ds(pl.multiple_of(me * slab, slab), slab)
 
     def scatter(t):
@@ -154,7 +155,8 @@
             ).start()
             return carry
 
-        lax.fori_loop(1, GROUPS, one, 0)
+        for k in far_first:
+            one(k, 0)
 
     for t in range(steps):
         scatter(t)
@@ -228,7 +230,7 @@
     def shared(t, i):
         share(t, i).wait_recv()
 
-    chunk = k_buf.shape[1]
+    chunk = v_buf.shape[2]
     v_buf[:, :, :, half:] = jnp.ones((2, 2, chunk, half), bf16)
     turn = [0]
 
@@ -236,23 +238,25 @@
         q = (dot(keys_in[t, pl.ds(0, block), :], wq[...]) * scale).astype(bf16)
         lane = lax.broadcasted_iota(jnp.int32, (block, width), 1) // head_dim
         for h in range(HEADS):
-            q_mask[t, h] = jnp.where(lane == h, q, jnp.zeros_like(q))
+            q_mask[t, h] = dot_t(jnp.where(lane == h, q, jnp.zeros_like(q)), wk[...]).astype(bf16)
 
     def attend(t, parts, fresh):
         slot = turn[0] % 2
         turn[0] += 1
         n = 0
+        cuts = []
         for start, count in parts:
             first_row = pl.multiple_of(start * block, block)
             rows_in = keys_in[t, pl.ds(first_row, count * block), :]
             here = pl.ds(n, count * block)
-            k_buf[slot, here, :] = dot(rows_in, wk[...]).astype(bf16)
+            cuts.append((first_row, count * block))
             v = dot(rows_in, wv[...]).astype(bf16)
             v_buf[slot, 0, here, :half] = v[:, :half]
             v_buf[slot, 1, here, :half] = v[:, half:]
             n += count * block
         for h in range(HEADS):
-            s = dot_t(q_mask[t, h], k_buf[slot, :n, :])
+            s = [dot_t(q_mask[t, h], keys_in[t, pl.ds(a, size), :]) for a, size in cuts]
+            s = s[0] if len(s) == 1 else jnp.concatenate(s, axis=1)
             top = jnp.max(s, axis=1, keepdims=True)
             if fresh:
                 new = jnp.broadcast_to(top, (block, 128))
@@ -294,7 +298,8 @@
             ).start()
             return carry
 
-        lax.fori_loop(1, GROUPS, one, 0)
+        for k in far_first:
+            one(k, 0)
 
     def near(t):
         def one(i, carry):
@@ -321,12 +326,12 @@
     project_queries(0)
     shared(0, 0)
     attend(0, [(0, 2)], True)
+    project_queries(1)
+    shared(1, 0)
+    attend(1, [(0, 2)], True)
     near_ready(0)
     own_ready(2)
-    project_queries(1)
     near(0)
-    shared(1, 0)
-    attend(1, [(0, 2)], True)
     side_ready(0)
     near_ready(1)
     project_queries(2)
@@ -402,7 +407,6 @@
             flat,
             pltpu.VMEM((window, slab, width), bf16),
             pltpu.VMEM((steps, BLOCK_SLOTS * block, width), bf16),
-            pltpu.VMEM((2, chunk, width), bf16),
             pltpu.VMEM((2, 2, chunk, width), bf16),
             pltpu.VMEM((steps, HEADS, block, width), bf16),
             pltpu.VMEM((steps, HEADS, block, width), f32),

time: 73.6 us -> 73.3 us (level)
  no operation moved by 1% of the time
where the time goes in v1:
time: 73.3 us; the launch traced here: 73.2 us
  Pallas kernels  71.4 us (97%)
  local copies, waits for them, and re-layouts  1.77 us (2%)
    pallas_call x1, Pallas kernels, shards(): pl.pallas_call(block_kernel, out_shape=jax.ShapeDtypeStruct(series.shape,...  71.4 us
    unnamed x1, local copies, waits for them, and re-layouts  1.77 us

profile of v1, /device:TPU:1, one launch (start us, length us, event | category | flops | bytes accessed | tf_op | source)
XLA Modules:
  0.0 73.2 jit_solution(11141444629428107116)
XLA Ops:
  0.0 71.4 %shard_map.109 = bf16[48,16,256]{2,1,0:T(8,128)(2,1)} custom-call(bf16[48,16,256]{2,1,0:T(8,128)(2,1)} %refs_0_.1, bf16[256,256]{1,0:T(8,128)(2,1)} %refs_1_.1, bf16[256,256]{1,0:T(8,128)(2,1)} %refs_2_.1, bf16[256,256]{1,0:T(8,128)(2,1)} %refs_3_.1, bf16[256,256]{1,0:T(8,128)(2,1)} %refs_4_.1, bf16[256,256]{1,0:T(8,128)(2,1)} %refs_5_.1, ...), custom_call_target="tpu_custom_call" | custom-call | tf_op jit(solution)/shard_map/pallas_call | solution.py:392
  71.4 1.8 %copy.13 = bf16[48,16,256]{2,1,0:T(8,128)(2,1)} copy(bf16[48,16,256]{2,1,0:T(8,128)(2,1)} %shard_map.109) | data formatting | bytes 786432
